TPU v7x, 32 devices: a whole 2x2x4 slice. The times are simulated.
32 devices in a mesh: member: 8 (over z, y), fsdp: 4 (over x, core).
Axes of the slice: x: 2, y: 2, z: 4, core: 2. Of those that a mesh axis runs over, the one named last changes fastest.
Arguments:
- probe_acts: bfloat16 [8, 4, 224, 4096], P('member', 'fsdp'), may hold values from -6 to 6
- member_weight: bfloat16 [8, 4096, 1792], P('member', 'fsdp'), may hold values from -6 to 6
- gate_values: bfloat16 [8, 4, 224, 1792], P('member', 'fsdp'), may hold values from -6 to 6
- out_grad: bfloat16 [8, 4, 224, 1792], P('member', 'fsdp'), may hold values from -6 to 6
- loss_mask: int32 [4, 224], P('fsdp'), may hold values 0 or 1
Outputs:
- merged: bfloat16 [4096, 1792], P(None, 'member')
- fisher_mean: float32 [4096, 1792], P('fsdp', 'member')
All inputs are finite; a program needn't handle non-finite values. No bound on the sum of `loss_mask` on one device may be relied on, other than what follows from the above.
Results may differ from a plain program's by a relative error of at most 0.0045.
Values may be sent and summed in bfloat16 or wider, within the bound.
A program may use at most 128 MiB of HBM per device.

v0:
```python
import jax
import jax.numpy as jnp
from jax import lax
from jax.sharding import PartitionSpec as P


def shards(probe_acts, member_weight, gate_values, out_grad, loss_mask):
    acts_local = probe_acts[0]
    weight_shard = member_weight[0]
    own_rows = weight_shard.shape[0]
    width_cols = weight_shard.shape[1]
    seq_len = acts_local.shape[1]
    gate_act = jax.nn.silu(gate_values[0].astype(jnp.float32))
    mask_float = loss_mask.astype(jnp.float32)[:, :, None]
    cotangent = (mask_float * out_grad[0].astype(jnp.float32) * gate_act).astype(jnp.bfloat16)
    columns = lax.all_to_all(acts_local, "fsdp", split_axis=2, concat_axis=0, tiled=True)
    norm_factor = 1.0 / (columns.shape[0] * seq_len)
    zeros_block = jnp.zeros((own_rows, width_cols), jnp.float32)
    all_cotangents = lax.all_gather(cotangent, "fsdp", axis=0, tiled=True)

    def add_example(index, acc):
        acts_one = lax.dynamic_index_in_dim(columns, 0 + index, 0, keepdims=False)
        cot_one = lax.dynamic_index_in_dim(all_cotangents, index, 0, keepdims=False)
        grads = jnp.einsum("lr,lc->rc", acts_one, cot_one, preferred_element_type=jnp.float32)
        return acc + grads * grads

    squares = lax.fori_loop(0, all_cotangents.shape[0], add_example, zeros_block)
    fisher = squares * norm_factor
    weighted_term = fisher * weight_shard.astype(jnp.float32)
    share_cols = width_cols // lax.axis_size("member")
    total_full, weighted_full = lax.psum((fisher, weighted_term), "member")
    first_col = lax.axis_index("member") * share_cols
    fisher_total = lax.dynamic_slice_in_dim(total_full, first_col, share_cols, 1)
    weighted = lax.dynamic_slice_in_dim(weighted_full, first_col, share_cols, 1)
    merged_part = (weighted / (fisher_total + 1e-06)).astype(jnp.bfloat16)
    merged = lax.all_gather(merged_part, "fsdp", axis=0, tiled=True)
    fisher_mean = fisher_total / lax.axis_size("member")
    return (merged, fisher_mean)


def solution(mesh):
    in_specs = (
        P("member", "fsdp", None, None),
        P("member", "fsdp", None),
        P("member", "fsdp", None, None),
        P("member", "fsdp", None, None),
        P("fsdp", None),
    )
    out_specs = (P(None, "member"), P("fsdp", "member"))
    return jax.shard_map(shards, mesh=mesh, in_specs=in_specs, out_specs=out_specs, check_vma=False)
```

profile of v0, /device:TPU:0, one launch (start us, length us, event | category | flops | bytes accessed | tf_op | source)
XLA Modules:
  0.0 622.8 jit_solution(4245465798634222640)
XLA Ops:
  7.2 0.8 convert_element_type.53
  8.0 2.8 fusion.9
  10.9 8.6 %copy.17 = bf16[1,224,4096]{1,0,2:T(2,128)(2,1)} copy(bf16[1,224,4096]{2,1,0:T(8,128)(2,1)S(1)} %bitcast.31) | data formatting | bytes 3670016 | tf_op jit(solution)/shard_map/squeeze | solution.py:8
  19.5 0.5 broadcast.46
  20.0 23.7 %reduce = bf16[4096,224]{1,0:T(8,128)(2,1)S(1)} reduce(bf16[4096,1,224]{2,1,0:T(2,128)(2,1)} %bitcast.27, bf16[]{:T(256)} %broadcast.46), dimensions={1}, to_apply=%bitcast.21.reduce_sub_computation | reduce | bytes 3670018
  43.7 4.3 reshape.97
  48.0 4.2 all-to-all-start
  52.2 5.9 copy.21
  58.2 17.0 %all-to-all-done = bf16[4,2,114688]{2,1,0:T(2,128)(2,1)S(1)} async-done(((bf16[4,2,114688]{2,1,0:T(2,128)(2,1)}), bf16[4,2,114688]{2,1,0:T(2,128)(2,1)S(1)}, u32[]{:S(2)}, u32[]{:S(2)}) %all-to-all-start) | async-done | bytes 1835040 | tf_op jit(solution)/shard_map/all_to_all | solution.py:16
  75.2 5.2 reshape.98
  80.3 2.5 copy.23
  82.9 2.4 copy.22
  85.3 2.0 copy.19
  87.4 27.7 %while.14 = (s32[]{:T(128)}, f32[1024,1792]{1,0:T(8,128)}, bf16[4,224,1024]{2,1,0:T(8,128)(2,1)S(1)}, bf16[4,224,1792]{2,1,0:T(8,128)(2,1)}, s32[]{:T(128)}, /*index=5*/s32[]{:T(128)}) while((s32[]{:T(128)}, f32[1024,1792]{1,0:T(8,128)}, bf16[4,224,1024]{2,1,0:T(8,128)(2,1)S(1)}, bf16[4,224,1792]{2,1,0:T(8,128)(2,1)}, s32[]{:T(128)}, ...), condition=%wide.region_1.2_spmd.clone, body=%wide.region_0.1_spmd.clone.sunk | while | flops 827588608 | bytes 15943254 | solution.py:27
  87.4 5.3 select_add_fusion.2
  92.7 7.5 %select_add_fusion.2 = f32[1024,1792]{1,0:T(8,128)} fusion(f32[1024,1792]{1,0:T(8,128)} %get-tuple-element.155, pred[]{:T(512)S(6)} %compare.3, bf16[4,224,1792]{2,1,0:T(8,128)(2,1)} %get-tuple-element.163, s32[]{:T(128)S(6)} %copy.26, bf16[4,224,1024]{2,1,0:T(8,128)(2,1)S(1)} %get-tuple-element.162), kind=kOutput, calls=%fused_computation.clone.1 | convolution fusion | flops 827588608 | bytes 15943168 | tf_op jit(solution)/shard_map/while/body/eval_jaxpr/lr,lc->rc/dot_general | solution.py:24
  100.1 7.5 %select_add_fusion.2 = f32[1024,1792]{1,0:T(8,128)} fusion(f32[1024,1792]{1,0:T(8,128)} %get-tuple-element.155, pred[]{:T(512)S(6)} %compare.3, bf16[4,224,1792]{2,1,0:T(8,128)(2,1)} %get-tuple-element.163, s32[]{:T(128)S(6)} %copy.26, bf16[4,224,1024]{2,1,0:T(8,128)(2,1)S(1)} %get-tuple-element.162), kind=kOutput, calls=%fused_computation.clone.1 | convolution fusion | flops 827588608 | bytes 15943168 | tf_op jit(solution)/shard_map/while/body/eval_jaxpr/lr,lc->rc/dot_general | solution.py:24
  107.6 7.5 %select_add_fusion.2 = f32[1024,1792]{1,0:T(8,128)} fusion(f32[1024,1792]{1,0:T(8,128)} %get-tuple-element.155, pred[]{:T(512)S(6)} %compare.3, bf16[4,224,1792]{2,1,0:T(8,128)(2,1)} %get-tuple-element.163, s32[]{:T(128)S(6)} %copy.26, bf16[4,224,1024]{2,1,0:T(8,128)(2,1)S(1)} %get-tuple-element.162), kind=kOutput, calls=%fused_computation.clone.1 | convolution fusion | flops 827588608 | bytes 15943168 | tf_op jit(solution)/shard_map/while/body/eval_jaxpr/lr,lc->rc/dot_general | solution.py:24
  115.1 8.4 %copy.20 = f32[1024,1792]{0,1:T(8,128)} copy(f32[1024,1792]{1,0:T(8,128)} %get-tuple-element.81) | data formatting | bytes 14680064 | tf_op jit(solution)/shard_map/while | solution.py:27
  123.5 12.1 %broadcast_multiply_fusion = (f32[1024,1792]{0,1:T(8,128)}, f32[1024,1792]{0,1:T(8,128)}) fusion(f32[1024,1792]{0,1:T(8,128)} %copy.20, bf16[1,1024,1792]{1,2,0:T(8,128)(2,1)} %copy.21), kind=kLoop, calls=%fused_computation.7 | loop fusion | flops 5505024 | bytes 25690112 | tf_op jit(solution)/shard_map/mul | solution.py:28
  135.7 454.5 %all-reduce.3.cloned.1.call-done = (f32[1024,1792]{0,1:T(8,128)}, f32[1024,1792]{0,1:T(8,128)}) async-done(((f32[1024,1792]{0,1:T(8,128)}, f32[1024,1792]{0,1:T(8,128)}), (f32[1024,1792]{0,1:T(8,128)}, f32[1024,1792]{0,1:T(8,128)})) %all-reduce.3.cloned.1.call-update) | async-done | bytes 14680080 | tf_op jit(solution)/shard_map/psum | solution.py:31
  590.2 2.8 dynamic-slice_multiply_fusion
  593.0 20.3 %all-gather.5.cloned.1.call-done = bf16[4096,224]{0,1:T(8,128)(2,1)} async-done(((bf16[1024,224]{0,1:T(8,128)(2,1)}), bf16[4096,224]{0,1:T(8,128)(2,1)}) %all-gather.5.cloned.1.call-update) | async-done | bytes 1835024 | tf_op jit(solution)/shard_map/all_gather | solution.py:36
  613.3 2.9 copy.33
  (10 shorter events, 0.2 us)
Async XLA Ops:
  7.2 3.7 copy-start
  7.2 80.2 %all-gather.3.cloned.1.call-start = ((), (), s32[]{:S(2)}) async-start(), calls=%async_computation.1 | async-start | bytes 4014080 | tf_op jit(solution)/shard_map/all_gather | solution.py:19
  48.0 27.2 %all-to-all-start = ((bf16[4,2,114688]{2,1,0:T(2,128)(2,1)}), bf16[4,2,114688]{2,1,0:T(2,128)(2,1)S(1)}, u32[]{:S(2)}, u32[]{:S(2)}) async-start(bf16[4,2,114688]{2,1,0:T(2,128)(2,1)} %reshape.97), calls=%async_computation | async-start | bytes 3670016 | tf_op jit(solution)/shard_map/all_to_all | solution.py:16
  52.2 538.0 %all-reduce.3.cloned.1.call-start = ((), (), s32[]{:S(2)}) async-start(), calls=%async_computation.3 | async-start | bytes 29360128 | tf_op jit(solution)/shard_map/psum | solution.py:31
  135.6 477.7 %all-gather.5.cloned.1.call-start = ((), (), s32[]{:S(2)}) async-start(), calls=%async_computation.2 | async-start | bytes 2293760 | tf_op jit(solution)/shard_map/all_gather | solution.py:36
Sparse Core Ops, SparseCore 0:
  11.0 31.5 all-gather.2
  135.8 454.4 all-reduce.2
  593.1 20.1 all-gather.4
where the time goes:
time: 623 us
  waiting for transfers between devices  492 us (79%)
  local copies, waits for them, and re-layouts  42.8 us (7%)
  other arithmetic  42.2 us (7%)
  matrix products  27.7 us (4%)
  between operations  13.8 us (2%)
    psum x1, waiting for transfers between devices, shards(): total_full, weighted_full = lax.psum((fisher, weighted_term), 'member')  455 us
    dot_general x4, matrix products, add_example(): jnp.einsum('lr,lc->rc', acts_one, cot_one, preferred_element_type=jnp.flo...  27.7 us
    unnamed x2, other arithmetic  23.7 us
    unnamed x9, local copies, waits for them, and re-layouts  23.5 us
    all_gather x1, waiting for transfers between devices, shards(): merged = lax.all_gather(merged_part, 'fsdp', axis=0, tiled=True)  20.3 us
    all_to_all x1, waiting for transfers between devices, shards(): lax.all_to_all(acts_local, 'fsdp', split_axis=2, concat_axis=0, tiled=True)  17 us
  transfers between devices with their start and end apart: 4, of which 3 were waited for; matrix products, arithmetic and copies ran while one was open for 9% of the time, Pallas kernels for 0%

commit v1 on v0

--- a/solution.py
+++ b/solution.py
@@ -13,7 +13,9 @@
     gate_act = jax.nn.silu(gate_values[0].astype(jnp.float32))
     mask_float = loss_mask.astype(jnp.float32)[:, :, None]
     cotangent = (mask_float * out_grad[0].astype(jnp.float32) * gate_act).astype(jnp.bfloat16)
-    columns = lax.all_to_all(acts_local, "fsdp", split_axis=2, concat_axis=0, tiled=True)
+    parts = jnp.split(acts_local, lax.axis_size("fsdp"), axis=2)
+    received = lax.all_to_all(jnp.stack(parts), "fsdp", 0, 0)
+    columns = jnp.concatenate(received, axis=0)
     norm_factor = 1.0 / (columns.shape[0] * seq_len)
     zeros_block = jnp.zeros((own_rows, width_cols), jnp.float32)
     all_cotangents = lax.all_gather(cotangent, "fsdp", axis=0, tiled=True)

time: 623 us -> 594 us (0.953)
  local copies, waits for them, and re-layouts: 42.8 us -> 17.5 us
  other arithmetic: 42.2 us -> 20 us
  waiting for transfers between devices: 492 us -> 511 us
    unnamed x2 -> x1, other arithmetic: 23.7 us -> 0.01 us
    all_to_all x1, waiting for transfers between devices: 17 us -> 33.3 us  [shards(): received = lax.all_to_all(jnp.stack(parts), 'fsdp', 0, 0)]
    unnamed x9 -> x4, local copies, waits for them, and re-layouts: 23.5 us -> 8.93 us
    squeeze x1 -> x0, local copies, waits for them, and re-layouts: 8.55 us -> none  [shards(): acts_local = probe_acts[0]]
  transfers between devices with their start and end apart: 4 -> 4, of which waited for: 3 -> 4; matrix products, arithmetic and copies ran while one was open for 9% -> 1% of each run, Pallas kernels for 0% -> 0%
where the time goes in v1:
time: 594 us
  waiting for transfers between devices  511 us (86%)
  matrix products  27.7 us (5%)
  other arithmetic  20 us (3%)
  local copies, waits for them, and re-layouts  17.5 us (3%)
  between operations  13.8 us (2%)
    psum x1, waiting for transfers between devices, shards(): total_full, weighted_full = lax.psum((fisher, weighted_term), 'member')  455 us
    all_to_all x1, waiting for transfers between devices, shards(): received = lax.all_to_all(jnp.stack(parts), 'fsdp', 0, 0)  33.3 us
    dot_general x4, matrix products, add_example(): jnp.einsum('lr,lc->rc', acts_one, cot_one, preferred_element_type=jnp.flo...  27.7 us
    all_gather x1, waiting for transfers between devices, shards(): merged = lax.all_gather(merged_part, 'fsdp', axis=0, tiled=True)  20.3 us
    mul x1, other arithmetic, shards(): fisher = squares * norm_factor  12.1 us
  transfers between devices with their start and end apart: 4, of which 4 were waited for; matrix products, arithmetic and copies ran while one was open for 1% of the time, Pallas kernels for 0%

profile of v1, /device:TPU:0, one launch (start us, length us, event | category | flops | bytes accessed | tf_op | source)
XLA Modules:
  0.0 593.9 jit_solution(10195035385518618891)
XLA Ops:
  7.2 0.0 all-gather.3.cloned.1.call-start
  7.2 0.8 convert_element_type.53
  8.0 2.8 fusion.9
  10.9 0.0 all-gather.3.cloned.1.call-update
  10.9 0.1 slice_bitcast_fusion.3
  11.1 1.5 pad_maximum_fusion
  12.5 4.2 all-to-all-start
  16.7 6.0 %copy.13 = bf16[1,1024,1792]{1,2,0:T(8,128)(2,1)} copy(bf16[1,1024,1792]{2,1,0:T(8,128)(2,1)} %param.8) | data formatting | bytes 7340032 | tf_op args[1]
  22.7 33.3 %all-to-all-done = bf16[4,1,224,1024]{3,2,1,0:T(8,128)(2,1)S(1)} async-done(((bf16[4,1,224,1024]{3,2,1,0:T(8,128)(2,1)}), bf16[4,1,224,1024]{3,2,1,0:T(8,128)(2,1)S(1)}, u32[]{:S(2)}, u32[]{:S(2)}) %all-to-all-start) | async-done | bytes 1835040 | tf_op jit(solution)/shard_map/all_to_all | solution.py:17
  56.0 2.4 all-gather.3.cloned.1.call-done
  58.4 27.7 %while.14 = (s32[]{:T(128)}, f32[1024,1792]{1,0:T(8,128)}, bf16[4,224,1024]{2,1,0:T(8,128)(2,1)S(1)}, bf16[4,224,1792]{2,1,0:T(8,128)(2,1)}, s32[]{:T(128)}, /*index=5*/s32[]{:T(128)}) while((s32[]{:T(128)}, f32[1024,1792]{1,0:T(8,128)}, bf16[4,224,1024]{2,1,0:T(8,128)(2,1)S(1)}, bf16[4,224,1792]{2,1,0:T(8,128)(2,1)}, s32[]{:T(128)}, ...), condition=%wide.region_1.2_spmd.clone, body=%wide.region_0.1_spmd.clone.sunk | while | flops 827588608 | bytes 15942735 | solution.py:29
  58.4 5.3 select_add_fusion.2
  63.7 7.5 %select_add_fusion.2 = f32[1024,1792]{1,0:T(8,128)} fusion(f32[1024,1792]{1,0:T(8,128)} %get-tuple-element.147, pred[]{:T(512)S(6)} %compare.3, bf16[4,224,1792]{2,1,0:T(8,128)(2,1)} %get-tuple-element.155, s32[]{:T(128)} %get-tuple-element.146, bf16[4,224,1024]{2,1,0:T(8,128)(2,1)S(1)} %get-tuple-element.154), kind=kOutput, calls=%fused_computation.clone.1 | convolution fusion | flops 827588608 | bytes 15942657 | tf_op jit(solution)/shard_map/while/body/eval_jaxpr/lr,lc->rc/dot_general | solution.py:26
  71.1 7.5 %select_add_fusion.2 = f32[1024,1792]{1,0:T(8,128)} fusion(f32[1024,1792]{1,0:T(8,128)} %get-tuple-element.147, pred[]{:T(512)S(6)} %compare.3, bf16[4,224,1792]{2,1,0:T(8,128)(2,1)} %get-tuple-element.155, s32[]{:T(128)} %get-tuple-element.146, bf16[4,224,1024]{2,1,0:T(8,128)(2,1)S(1)} %get-tuple-element.154), kind=kOutput, calls=%fused_computation.clone.1 | convolution fusion | flops 827588608 | bytes 15942657 | tf_op jit(solution)/shard_map/while/body/eval_jaxpr/lr,lc->rc/dot_general | solution.py:26
  78.6 7.5 %select_add_fusion.2 = f32[1024,1792]{1,0:T(8,128)} fusion(f32[1024,1792]{1,0:T(8,128)} %get-tuple-element.147, pred[]{:T(512)S(6)} %compare.3, bf16[4,224,1792]{2,1,0:T(8,128)(2,1)} %get-tuple-element.155, s32[]{:T(128)} %get-tuple-element.146, bf16[4,224,1024]{2,1,0:T(8,128)(2,1)S(1)} %get-tuple-element.154), kind=kOutput, calls=%fused_computation.clone.1 | convolution fusion | flops 827588608 | bytes 15942657 | tf_op jit(solution)/shard_map/while/body/eval_jaxpr/lr,lc->rc/dot_general | solution.py:26
  86.1 8.4 %copy.12 = f32[1024,1792]{0,1:T(8,128)} copy(f32[1024,1792]{1,0:T(8,128)} %get-tuple-element.81) | data formatting | bytes 14680064 | tf_op jit(solution)/shard_map/while | solution.py:29
  94.4 12.1 %broadcast_multiply_fusion = (f32[1024,1792]{0,1:T(8,128)}, f32[1024,1792]{0,1:T(8,128)}) fusion(f32[1024,1792]{0,1:T(8,128)} %copy.12, bf16[1,1024,1792]{1,2,0:T(8,128)(2,1)} %copy.13), kind=kLoop, calls=%fused_computation.7 | loop fusion | flops 5505024 | bytes 25690112 | tf_op jit(solution)/shard_map/mul | solution.py:30
  106.6 0.0 all-reduce.3.cloned.1.call-update
  106.6 0.0 all-gather.5.cloned.1.call-start
  106.7 454.6 %all-reduce.3.cloned.1.call-done = (f32[1024,1792]{0,1:T(8,128)}, f32[1024,1792]{0,1:T(8,128)}) async-done(((f32[1024,1792]{0,1:T(8,128)}, f32[1024,1792]{0,1:T(8,128)}), (f32[1024,1792]{0,1:T(8,128)}, f32[1024,1792]{0,1:T(8,128)})) %all-reduce.3.cloned.1.call-update) | async-done | bytes 14680080 | tf_op jit(solution)/shard_map/psum | solution.py:33
  561.3 2.8 dynamic-slice_multiply_fusion
  564.1 0.0 all-gather.5.cloned.1.call-update
  564.1 20.3 %all-gather.5.cloned.1.call-done = bf16[4096,224]{0,1:T(8,128)(2,1)} async-done(((bf16[1024,224]{0,1:T(8,128)(2,1)}), bf16[4096,224]{0,1:T(8,128)(2,1)}) %all-gather.5.cloned.1.call-update) | async-done | bytes 1835024 | tf_op jit(solution)/shard_map/all_gather | solution.py:38
  584.4 2.9 copy.23
  (4 shorter events, 0.0 us)
Async XLA Ops:
  7.2 3.7 copy-start
  7.2 51.2 %all-gather.3.cloned.1.call-start = ((), (), s32[]{:S(2)}) async-start(), calls=%async_computation.1 | async-start | bytes 4014080 | tf_op jit(solution)/shard_map/all_gather | solution.py:21
  12.5 43.5 %all-to-all-start = ((bf16[4,1,224,1024]{3,2,1,0:T(8,128)(2,1)}), bf16[4,1,224,1024]{3,2,1,0:T(8,128)(2,1)S(1)}, u32[]{:S(2)}, u32[]{:S(2)}) async-start(bf16[4,1,224,1024]{3,2,1,0:T(8,128)(2,1)} %pad_maximum_fusion), calls=%async_computation | async-start | bytes 3670016 | tf_op jit(solution)/shard_map/all_to_all | solution.py:17
  16.7 544.6 %all-reduce.3.cloned.1.call-start = ((), (), s32[]{:S(2)}) async-start(), calls=%async_computation.3 | async-start | bytes 29360128 | tf_op jit(solution)/shard_map/psum | solution.py:33
  106.6 477.8 %all-gather.5.cloned.1.call-start = ((), (), s32[]{:S(2)}) async-start(), calls=%async_computation.2 | async-start | bytes 2293760 | tf_op jit(solution)/shard_map/all_gather | solution.py:38
Sparse Core Ops, SparseCore 0:
  11.0 47.3 all-gather.2
  106.7 454.5 all-reduce.2
  564.2 20.1 all-gather.4
